TPU v7x, 128 devices: a whole 4x4x4 slice. The times are simulated.
128 devices in a mesh: train: 32 (over z, y_lo, x), tp: 4 (over y_hi, core).
Axes of the slice: x: 4, y: 4 (y_hi: 2, y_lo: 2; y = y_hi * 2 + y_lo), z: 4, core: 2. Of those that a mesh axis runs over, the one named last changes fastest.
Arguments:
- offsets: int32 [3], replicated, may hold values from 1 to 127
- gate_flat: float32 [4, 44040192], P('tp', 'train'), may hold values from -0.0546875 to 0.0546875
- up_flat: float32 [4, 44040192], P('tp', 'train'), may hold values from -0.0546875 to 0.0546875
- down_flat: float32 [4, 44040192], P('tp', 'train'), may hold values from -0.046875 to 0.046875
- norm_gain: float32 [12288], replicated, may hold values from 0.1 to 1.9
- decode_state: bfloat16 [256, 12288], P(None, 'train'), may hold values from -33 to 33
Outputs:
- gate_codes: bfloat16 [14336, 12288], P('tp', 'train')
- gate_scales: float32 [14336, 96], P('tp', 'train')
- up_codes: bfloat16 [14336, 12288], P('tp', 'train')
- up_scales: float32 [14336, 96], P('tp', 'train')
- down_codes: bfloat16 [12288, 14336], P('train', 'tp')
- down_scales: float32 [12288, 112], P('train', 'tp')
- decoded: bfloat16 [256, 12288], P(None, 'train')
All inputs are finite; a program needn't handle non-finite values. Where the computation divides by a largest or mean magnitude, that divisor is 1e-20 or more.
Results may differ from a plain program's by a relative error of at most 0.025.
Values may be sent and summed in bfloat16 or wider, within the bound.
No kernel may reach another device: no remote copies, remote signals or barrier semaphores. Data moves between devices by JAX's collectives and lax.ppermute only.
A program may use at most 192 MiB of HBM per device.

v0:
```python
import jax
import jax.numpy as jnp
from jax import lax
from jax.sharding import PartitionSpec as P

GROUP = 128
STEPS = 3


EPSILON_SCALE = 1e-06
EPSILON_NORM = 1e-05


def shifted(block, axis, distance):
    devices = range(lax.axis_size(axis))
    route = [((i - distance) % len(devices), i) for i in devices]
    return lax.ppermute(block, axis, route)


def quantize(matrix):
    count_rows, count_cols = matrix.shape
    grouped = matrix.reshape(count_rows, count_cols // GROUP, GROUP)
    scales = jnp.max(jnp.abs(grouped), axis=2) + EPSILON_SCALE
    codes = (grouped / scales[:, :, None]).astype(jnp.bfloat16)
    return (codes.reshape(count_rows, count_cols), scales)


def dequantize(codes, scales):
    count_rows, count_cols = codes.shape
    grouped = codes.astype(jnp.float32).reshape(count_rows, count_cols // GROUP, GROUP)
    return (grouped * scales[:, :, None]).astype(jnp.bfloat16).reshape(count_rows, count_cols)


def realign(buffer, following, start, count_rows):
    joined = jnp.concatenate([buffer[0], following])
    return lax.dynamic_slice_in_dim(joined, start, buffer.shape[1], 0).reshape(count_rows, -1)


def body(offsets, gate_flat, up_flat, down_flat, norm_gain, decode_state):
    model_width = norm_gain.shape[0]
    part_width = decode_state.shape[1]
    token_count = decode_state.shape[0]
    shard_rows = gate_flat.shape[1] // model_width
    contraction = (((1,), (1,)), ((), ()))
    heads = (gate_flat[0, :GROUP], up_flat[0, :GROUP], down_flat[0, :GROUP])
    following = shifted((heads[0], heads[1], heads[2]), "train", -1)
    gate_rows = realign(gate_flat, following[0], offsets[0], shard_rows)
    up_rows = realign(up_flat, following[1], offsets[1], shard_rows)
    down_rows = realign(down_flat, following[2], offsets[2], part_width)
    down_codes, down_scales = quantize(down_rows)
    down_served = dequantize(down_codes, down_scales)
    gate_owned, up_owned = (
        lax.all_to_all(gate_rows, "train", split_axis=1, concat_axis=0, tiled=True),
        lax.all_to_all(up_rows, "train", split_axis=1, concat_axis=0, tiled=True),
    )
    gate_codes, gate_scales = quantize(gate_owned)
    up_codes, up_scales = quantize(up_owned)
    gate_served = dequantize(gate_codes, gate_scales)
    up_served = dequantize(up_codes, up_scales)
    gain_part = lax.dynamic_slice_in_dim(
        norm_gain, lax.axis_index("train") * part_width, part_width, 0
    )
    state = decode_state
    for step in range(STEPS):
        wide_state = state.astype(jnp.float32)
        squares = lax.psum(jnp.sum(wide_state * wide_state, axis=1), "train")
        scaled_part = (wide_state * gain_part[None, :]).astype(jnp.bfloat16)
        gate_term = lax.dot_general(
            gate_served, scaled_part, contraction, preferred_element_type=jnp.float32
        )
        up_term = lax.dot_general(
            up_served, scaled_part, contraction, preferred_element_type=jnp.float32
        )
        shares = lax.psum_scatter(
            jnp.concatenate([gate_term, up_term], axis=1), "train", scatter_dimension=0, tiled=True
        )
        gate_sums = shares[:, :token_count]
        up_sums = shares[:, token_count:]
        inverse = lax.rsqrt(squares / model_width + EPSILON_NORM)
        hidden = (jax.nn.silu(gate_sums * inverse[None, :]) * (up_sums * inverse[None, :])).astype(
            jnp.bfloat16
        )
        partial_update = lax.dot_general(
            lax.all_gather(hidden, "train", axis=0, tiled=True),
            down_served,
            (((0,), (1,)), ((), ())),
            preferred_element_type=jnp.float32,
        )
        update = lax.psum(partial_update, "tp")
        state = (state.astype(jnp.float32) + update).astype(jnp.bfloat16)
    return (gate_codes, gate_scales, up_codes, up_scales, down_codes, down_scales, state)


def solution(mesh):
    in_specs = (P(), P("tp", "train"), P("tp", "train"), P("tp", "train"), P(), P(None, "train"))
    out_specs = (
        P("tp", "train"),
        P("tp", "train"),
        P("tp", "train"),
        P("tp", "train"),
        P("train", "tp"),
        P("train", "tp"),
        P(None, "train"),
    )
    return jax.shard_map(body, mesh=mesh, in_specs=in_specs, out_specs=out_specs, check_vma=False)
```

profile of v0, /device:TPU:1, one launch (start us, length us, event | category | flops | bytes accessed | tf_op | source)
XLA Modules:
  0.0 1432.4 jit_solution(3245126900498138564)
XLA Ops:
  7.8 7.8 collective-permute-start.1
  35.9 8.1 copy.34
  62.9 8.2 copy.31
  71.1 49.9 %all-to-all-done.1 = f32[112,32,384]{2,0,1:T(8,128)} async-done(((f32[112,32,384]{2,0,1:T(8,128)}), f32[112,32,384]{2,0,1:T(8,128)}, u32[]{:S(2)}, u32[]{:S(2)}) %all-to-all-start.1) | async-done | bytes 5505056 | tf_op jit(solution)/shard_map/all_to_all | solution.py:54
  121.0 13.1 all-to-all-start
  140.3 9.3 reshape.78
  166.9 38.0 %all-to-all-done = f32[112,32,384]{2,0,1:T(8,128)} async-done(((f32[112,32,384]{2,0,1:T(8,128)}), f32[112,32,384]{2,0,1:T(8,128)}, u32[]{:S(2)}, u32[]{:S(2)}) %all-to-all-start) | async-done | bytes 5505056 | tf_op jit(solution)/shard_map/all_to_all | solution.py:53
  210.4 9.1 reshape.77
  257.7 8.4 copy.48
  270.1 68.8 %psum.42 = f32[256]{0:T(256)S(1)} all-reduce(f32[256]{0:T(256)S(1)} %fusion.6), channel_id=1, replica_groups=mesh['train'=32,'tp'=4] {'train'}, use_global_device_ids=true, to_apply=%region_5.0 | all-reduce | flops 256 | bytes 2048 | tf_op jit(solution)/shard_map/psum | solution.py:66
  338.9 85.7 %reduce-scatter.10.cloned.1.call-done = f32[112,512]{1,0:T(8,128)} async-done(((f32[3584,512]{1,0:T(8,128)}), f32[112,512]{1,0:T(8,128)}) %reduce-scatter.10.cloned.1.call-update) | async-done | bytes 229392
  461.3 7.8 multiply_convert_fusion
  469.1 109.4 %all-gather.4.cloned.1.call-done = bf16[3584,256]{1,0:T(8,128)(2,1)} async-done(((bf16[112,256]{1,0:T(8,128)(2,1)}), bf16[3584,256]{1,0:T(8,128)(2,1)}) %all-gather.4.cloned.1.call-update) | async-done | bytes 1835024 | tf_op jit(solution)/shard_map/all_gather | solution.py:84
  582.8 62.3 %all-reduce.4.cloned.1.call-done = f32[256,384]{1,0:T(8,128)} async-done(((f32[256,384]{1,0:T(8,128)}), f32[256,384]{1,0:T(8,128)}) %all-reduce.4.cloned.1.call-update) | async-done | bytes 393232 | tf_op jit(solution)/shard_map/psum | solution.py:89
  652.2 8.4 copy.50
  660.7 70.2 %psum.44 = f32[256]{0:T(256)S(1)} all-reduce(f32[256]{0:T(256)S(1)} %get-tuple-element.23), channel_id=1, replica_groups=mesh['train'=32,'tp'=4] {'train'}, use_global_device_ids=true, to_apply=%region_9.10 | all-reduce | flops 256 | bytes 2048 | tf_op jit(solution)/shard_map/psum | solution.py:66
  730.9 82.5 %reduce-scatter.12.cloned.1.call-done = f32[112,512]{1,0:T(8,128)} async-done(((f32[3584,512]{1,0:T(8,128)}), f32[112,512]{1,0:T(8,128)}) %reduce-scatter.12.cloned.1.call-update) | async-done | bytes 229392
  815.5 152.8 %all-gather.6.cloned.1.call-done = bf16[3584,256]{1,0:T(8,128)(2,1)} async-done(((bf16[112,256]{1,0:T(8,128)(2,1)}), bf16[3584,256]{1,0:T(8,128)(2,1)}) %all-gather.6.cloned.1.call-update) | async-done | bytes 1835024 | tf_op jit(solution)/shard_map/all_gather | solution.py:84
  973.0 62.0 %all-reduce.6.cloned.1.call-done = f32[256,384]{1,0:T(8,128)} async-done(((f32[256,384]{1,0:T(8,128)}), f32[256,384]{1,0:T(8,128)}) %all-reduce.6.cloned.1.call-update) | async-done | bytes 393232 | tf_op jit(solution)/shard_map/psum | solution.py:89
  1042.1 8.4 copy.52
  1050.6 71.1 %psum.46 = f32[256]{0:T(256)S(1)} all-reduce(f32[256]{0:T(256)S(1)} %get-tuple-element.21), channel_id=1, replica_groups=mesh['train'=32,'tp'=4] {'train'}, use_global_device_ids=true, to_apply=%region_13.14 | all-reduce | flops 256 | bytes 2048 | tf_op jit(solution)/shard_map/psum | solution.py:66
  1121.7 81.4 %reduce-scatter.14.cloned.1.call-done = f32[112,512]{1,0:T(8,128)} async-done(((f32[3584,512]{1,0:T(8,128)}), f32[112,512]{1,0:T(8,128)}) %reduce-scatter.14.cloned.1.call-update) | async-done | bytes 229392
  1205.2 152.6 %all-gather.8.cloned.1.call-done = bf16[3584,256]{1,0:T(8,128)(2,1)} async-done(((bf16[112,256]{1,0:T(8,128)(2,1)}), bf16[3584,256]{1,0:T(8,128)(2,1)}) %all-gather.8.cloned.1.call-update) | async-done | bytes 1835024 | tf_op jit(solution)/shard_map/all_gather | solution.py:84
  1361.2 62.4 %all-reduce.8.cloned.1.call-done = f32[256,384]{1,0:T(8,128)} async-done(((f32[256,384]{1,0:T(8,128)}), f32[256,384]{1,0:T(8,128)}) %all-reduce.8.cloned.1.call-update) | async-done | bytes 393232 | tf_op jit(solution)/shard_map/psum | solution.py:89
  (107 shorter events, 174.3 us)
Async XLA Ops:
  7.8 14.2 collective-permute-start.1
  16.3 32.8 %collective-permute-start = (f32[128]{0:T(128)S(1)}, f32[128]{0:T(128)S(1)}, u32[]{:S(2)}, u32[]{:S(2)}) collective-permute-start(f32[128]{0:T(128)S(1)} %slice_bitcast_fusion.2), channel_id=1, source_target_pairs={{4,0},{8,4},{12,8},{16,12},{20,16},{24,20},{28,24},{32,28},{36,32}... | collective-permute-start | bytes 1544 | tf_op jit(solution)/shard_map/ppermute | solution.py:17
  44.0 76.9 %all-to-all-start.1 = ((f32[112,32,384]{2,0,1:T(8,128)}), f32[112,32,384]{2,0,1:T(8,128)}, u32[]{:S(2)}, u32[]{:S(2)}) async-start(f32[112,32,384]{2,0,1:T(8,128)} %copy.34), calls=%async_computation.1 | async-start | bytes 11010048 | tf_op jit(solution)/shard_map/all_to_all | solution.py:54
  121.0 84.0 %all-to-all-start = ((f32[112,32,384]{2,0,1:T(8,128)}), f32[112,32,384]{2,0,1:T(8,128)}, u32[]{:S(2)}, u32[]{:S(2)}) async-start(f32[112,32,384]{2,0,1:T(8,128)} %copy.31), calls=%async_computation | async-start | bytes 11010048 | tf_op jit(solution)/shard_map/all_to_all | solution.py:53
  134.1 290.5 %reduce-scatter.10.cloned.1.call-start = ((), (), s32[]{:S(2)}) async-start(), calls=%async_computation.11 | async-start | bytes 7569408
  157.7 9.2 copy-start.6
  227.6 9.2 copy-start.7
  236.8 6.8 copy-start.4
  243.6 2.6 copy-start.3
  251.5 1.5 copy-start
  266.1 312.4 %all-gather.4.cloned.1.call-start = ((), (), s32[]{:S(2)}) async-start(), calls=%async_computation.5 | async-start | bytes 1892352 | tf_op jit(solution)/shard_map/all_gather | solution.py:84
  266.8 159.8 %collective-permute-start.2 = (f32[128]{0:T(128)S(1)}, f32[128]{0:T(128)S(1)}, u32[]{:S(2)}, u32[]{:S(2)}) collective-permute-start(f32[128]{0:T(128)S(1)} %slice_bitcast_fusion), channel_id=1, source_target_pairs={{4,0},{8,4},{12,8},{16,12},{20,16},{24,20},{28,24},{32,28},{36,32}... | collective-permute-start | bytes 1544 | tf_op jit(solution)/shard_map/ppermute | solution.py:17
  426.6 218.5 %all-reduce.4.cloned.1.call-start = ((), (), s32[]{:S(2)}) async-start(), calls=%async_computation.6 | async-start | bytes 786432 | tf_op jit(solution)/shard_map/psum | solution.py:89
  445.7 8.9 copy-start.8
  582.8 230.7 %reduce-scatter.12.cloned.1.call-start = ((), (), s32[]{:S(2)}) async-start(), calls=%async_computation.12 | async-start | bytes 7569408
  645.1 2.4 copy-start.1
  660.6 307.7 %all-gather.6.cloned.1.call-start = ((), (), s32[]{:S(2)}) async-start(), calls=%async_computation.7 | async-start | bytes 1892352 | tf_op jit(solution)/shard_map/all_gather | solution.py:84
  815.5 219.6 %all-reduce.6.cloned.1.call-start = ((), (), s32[]{:S(2)}) async-start(), calls=%async_computation.8 | async-start | bytes 786432 | tf_op jit(solution)/shard_map/psum | solution.py:89
  972.7 230.4 %reduce-scatter.14.cloned.1.call-start = ((), (), s32[]{:S(2)}) async-start(), calls=%async_computation.13 | async-start | bytes 7569408
  1035.0 2.4 copy-start.2
  1050.5 307.2 %copy-start.5 = (bf16[384,3584]{1,0:T(8,128)(2,1)S(1)}, bf16[384,3584]{1,0:T(8,128)(2,1)}, u32[]{:S(2)}) copy-start(bf16[384,3584]{1,0:T(8,128)(2,1)} %get-tuple-element.25) | copy-start | bytes 8257540
  1050.5 307.2 %all-gather.8.cloned.1.call-start = ((), (), s32[]{:S(2)}) async-start(), calls=%async_computation.9 | async-start | bytes 1892352 | tf_op jit(solution)/shard_map/all_gather | solution.py:84
  1205.1 218.5 %all-reduce.8.cloned.1.call-start = ((), (), s32[]{:S(2)}) async-start(), calls=%async_computation.10 | async-start | bytes 786432 | tf_op jit(solution)/shard_map/psum | solution.py:89
Sparse Core Ops, SparseCore 0:
  266.2 158.2 reduce-scatter.9
  426.8 151.6 all-gather.3
  582.9 62.2 all-reduce.3
  660.7 152.6 reduce-scatter.11
  815.6 152.7 all-gather.5
  972.8 62.2 all-reduce.5
  1050.7 152.3 reduce-scatter.13
  1205.3 152.4 all-gather.7
  1361.4 62.2 all-reduce.7
where the time goes:
time: 1440 us; the launch traced here: 1430 us
  waiting for transfers between devices  939 us (65%)
  blocking collectives  210 us (15%)
  local copies, waits for them, and re-layouts  129 us (9%)
  other arithmetic  86.8 us (6%)
  starting transfers between devices  28.4 us (2%)
  between operations  20.5 us (1%)
  matrix products  18.9 us (1%)
    all_gather x3, waiting for transfers between devices, body(): lax.all_gather(hidden, 'train', axis=0, tiled=True)  415 us
    unnamed x12, waiting for transfers between devices  250 us
    psum x3, blocking collectives, body(): squares = lax.psum(jnp.sum(wide_state * wide_state, axis=1), 'train')  210 us
    psum x3, waiting for transfers between devices, body(): update = lax.psum(partial_update, 'tp')  187 us
    all_to_all x1, waiting for transfers between devices, body(): lax.all_to_all(up_rows, 'train', split_axis=1, concat_axis=0, tiled=True)  49.9 us
    all_to_all x1, waiting for transfers between devices, body(): lax.all_to_all(gate_rows, 'train', split_axis=1, concat_axis=0, tiled=True)  38 us
    unnamed x29, local copies, waits for them, and re-layouts  29.8 us
  transfers between devices with their start and end apart: 14, of which 11 were waited for; matrix products, arithmetic and copies ran while one was open for 8% of the time, Pallas kernels for 0%

commit v1 on v0

v1 whole, which is shorter than its diff:
```python
import functools

import jax
import jax.numpy as jnp
from jax import lax
from jax.experimental import pallas as pl
from jax.experimental.pallas import tpu as pltpu
from jax.sharding import PartitionSpec as P

GROUP = 128
STEPS = 3
EPSILON_SCALE = 1e-06
EPSILON_NORM = 1e-05

N_Z = 4
N_Q = 8
N_TRAIN = N_Z * N_Q
ROWS = 112
PART = 384
PER = PART // GROUP
GROUPS_ROW = N_TRAIN * PER
BLOCK = 16
STRIP = 2 * ROWS + BLOCK
FT = ROWS * N_TRAIN
DOWN_GROUPS = FT // GROUP
DOWN_PER = DOWN_GROUPS // N_Z
DOWN_BLOCK = 64
DOWN_BLOCKS = PART // DOWN_BLOCK
TOK = 256
MSG = PART + BLOCK
VMEM_LIMIT = 28 * 1024 * 1024
HALF = TOK // 2
Z_HALF = N_Z // 2

bf16, f32 = jnp.bfloat16, jnp.float32


def params():
    return pltpu.CompilerParams(vmem_limit_bytes=VMEM_LIMIT)


def lanes_of(shape):
    return lax.broadcasted_iota(jnp.int32, shape, len(shape) - 1)


def following_rows(first, follow, turn):
    count = first.shape[0]
    up = pltpu.roll(first, count - 1, axis=0)
    row = lax.broadcasted_iota(jnp.int32, first.shape, 0)
    return pltpu.roll(jnp.where(row == count - 1, follow, up), turn, axis=1)


def realigned(x_ref, follow, turn, count, stride):
    lane = lanes_of((count, GROUP))
    own = lane < turn
    first = x_ref[pl.ds(0, count, stride=stride), :]
    current = pltpu.roll(first, turn, axis=1)
    for g in range(stride):
        if g + 1 < stride:
            after = pltpu.roll(x_ref[pl.ds(g + 1, count, stride=stride), :], turn, axis=1)
        else:
            after = following_rows(first, follow, turn)
        yield g, jnp.where(own, current, after)
        current = after


def scaled_group(group):
    scale = jnp.max(jnp.abs(group), axis=1, keepdims=True) + EPSILON_SCALE
    return scale, (group * (1.0 / scale)).astype(bf16)


def follow_of(step, last, next_ref, heads_ref, index):
    return jnp.where(step == last, heads_ref[index : index + 1, :], next_ref[0:1, :])


def pack_kernel(
    z_first, off_ref, gate_ref, gate_next, up_ref, up_next, heads_ref, out_ref, served_ref, kept_all, parts, rows
):
    step = pl.program_id(0)
    lane = lanes_of((ROWS, GROUP))
    last = (step == Z_HALF - 1) & (z_first > 0)
    kept_all[...] = jnp.zeros_like(kept_all)
    rows[...] = jnp.zeros_like(rows)
    for index, (x_ref, next_ref) in enumerate(((gate_ref, gate_next), (up_ref, up_next))):
        turn = GROUP - off_ref[index]
        own = lane < turn

        def turned(block):
            return pltpu.roll(block, turn, axis=1)

        after_row = next_ref[:, 0, :]
        wrapped = pltpu.roll(after_row, ROWS - 1, axis=0)
        row = lax.broadcasted_iota(jnp.int32, after_row.shape, 0)
        wrapped = jnp.where(row == ROWS - 1, heads_ref[index : index + 1, :], wrapped)
        follow = jnp.where(last, wrapped, after_row)
        kept = jnp.zeros((ROWS, GROUP), f32)
        current = turned(x_ref[:, 0, :])
        for g in range(N_Q * PER):
            after = turned(x_ref[:, g + 1, :] if g + 1 < N_Q * PER else follow)
            scale, codes = scaled_group(jnp.where(own, current, after))
            current = after
            q, k = g // PER, g % PER
            out_ref[q, 0, index * ROWS : (index + 1) * ROWS, k * GROUP : (k + 1) * GROUP] = codes
            served_ref[index * ROWS : (index + 1) * ROWS, g * GROUP : (g + 1) * GROUP] = (
                codes.astype(f32) * scale
            ).astype(bf16)
            kept = jnp.where(lane == q * 4 + k, scale, kept)
        kept_all[:ROWS, :] = kept
        rest = kept_all[...].T
        for part in range(3):
            piece = rest.astype(bf16).astype(f32)
            rest = rest - piece
            parts[...] = piece
            for k in range(PER):
                rows[k, pl.ds(index * 3 + part, N_Q, stride=BLOCK), :] = parts[pl.ds(k, N_Q, stride=4), :]
    for k in range(PER):
        out_ref[:, 0, 2 * ROWS :, k * GROUP : (k + 1) * GROUP] = (
            rows[k].reshape(N_Q, BLOCK, GROUP).astype(bf16)
        )


def pack(z_first, offsets, gate, up, heads):
    gate, up = (flat.reshape(ROWS, GROUPS_ROW, GROUP) for flat in (gate, up))
    part = N_Q * PER
    main = pl.BlockSpec((ROWS, part, GROUP), lambda s, off: (0, s + z_first, 0))
    after = pl.BlockSpec((ROWS, 8, GROUP), lambda s, off: (0, lax.rem((s + z_first + 1) * (part // 8), GROUPS_ROW // 8), 0))
    return pl.pallas_call(
        functools.partial(pack_kernel, z_first),
        out_shape=(
            jax.ShapeDtypeStruct((N_Q, Z_HALF, STRIP, PART), bf16),
            jax.ShapeDtypeStruct((2 * ROWS, Z_HALF * part * GROUP), bf16),
        ),
        grid_spec=pltpu.PrefetchScalarGridSpec(
            num_scalar_prefetch=1,
            grid=(Z_HALF,),
            in_specs=[main, after, main, after, pl.BlockSpec((8, GROUP), lambda s, off: (0, 0))],
            out_specs=(
                pl.BlockSpec((N_Q, 1, STRIP, PART), lambda s, off: (0, s, 0, 0)),
                pl.BlockSpec((2 * ROWS, part * GROUP), lambda s, off: (0, s)),
            ),
            scratch_shapes=[
                pltpu.VMEM((GROUP, GROUP), f32),
                pltpu.VMEM((GROUP, GROUP), f32),
                pltpu.VMEM((PER, N_Q * BLOCK, GROUP), f32),
            ],
        ),
        compiler_params=params(),
        name="pack_gate_up",
    )(offsets, gate, gate, up, up, heads)


def down_code_kernel(off_ref, place_ref, x_ref, next_ref, heads_ref, codes_ref, scales_ref, served_ref):
    step = pl.program_id(0)
    turn = GROUP - off_ref[2]
    follow = follow_of(step, DOWN_BLOCKS - 1, next_ref, heads_ref, 2)
    lane = lanes_of((DOWN_BLOCK, GROUP))
    kept = jnp.zeros((DOWN_BLOCK, GROUP), f32)
    for g, group in realigned(x_ref, follow, turn, DOWN_BLOCK, DOWN_GROUPS):
        scale, codes = scaled_group(group)
        codes_ref[:, g * GROUP : (g + 1) * GROUP] = codes
        z, k = g // DOWN_PER, g % DOWN_PER
        served_ref[lax.rem(z - place_ref[0] + N_Z, N_Z), :, k * GROUP : (k + 1) * GROUP] = (
            codes.astype(f32) * scale
        ).astype(bf16)
        kept = jnp.where(lane == g, scale, kept)
    scales_ref[...] = kept[:, :DOWN_GROUPS]


def code_down(offsets, place, down, heads):
    block_groups = DOWN_BLOCK * DOWN_GROUPS
    last = PART * DOWN_GROUPS // 8 - 1
    return pl.pallas_call(
        down_code_kernel,
        out_shape=(
            jax.ShapeDtypeStruct((PART, FT), bf16),
            jax.ShapeDtypeStruct((PART, DOWN_GROUPS), f32),
            jax.ShapeDtypeStruct((N_Z, PART, FT // N_Z), bf16),
        ),
        grid_spec=pltpu.PrefetchScalarGridSpec(
            num_scalar_prefetch=2,
            grid=(DOWN_BLOCKS,),
            in_specs=[
                pl.BlockSpec((block_groups, GROUP), lambda s, *_: (s, 0)),
                pl.BlockSpec((8, GROUP), lambda s, *_: (jnp.minimum((s + 1) * (block_groups // 8), last), 0)),
                pl.BlockSpec((8, GROUP), lambda s, *_: (0, 0)),
            ],
            out_specs=(
                pl.BlockSpec((DOWN_BLOCK, FT), lambda s, *_: (s, 0)),
                pl.BlockSpec((DOWN_BLOCK, DOWN_GROUPS), lambda s, *_: (s, 0)),
                pl.BlockSpec((N_Z, DOWN_BLOCK, FT // N_Z), lambda s, *_: (0, s, 0)),
            ),
        ),
        compiler_params=params(),
        name="code_down",
    )(offsets, place, down, down, heads)


def scale_columns(strip_of, count, gathered):
    gathered[...] = jnp.zeros_like(gathered)
    for n in range(count):
        tail = strip_of(n).astype(f32)
        for index in range(2):
            row = tail[3 * index : 3 * index + 1] + tail[3 * index + 1 : 3 * index + 2]
            row = row + tail[3 * index + 2 : 3 * index + 3]
            for k in range(PER):
                at = (n * 2 + index) * PER + k
                gathered[at : at + 1, :] = row[:, k * GROUP : (k + 1) * GROUP]
    return gathered[...].T


def serve_kernel(place_ref, in_ref, *refs):
    served_ref, gate_ref, up_ref, gathered = refs[-4:]
    columns = scale_columns(lambda n: in_ref[0, n, 2 * ROWS : STRIP, :], Z_HALF, gathered)
    for z in range(Z_HALF):
        gate_ref[z, 0] = in_ref[0, z, :ROWS]
        up_ref[z, 0] = in_ref[0, z, ROWS:]
        for index in range(2):
            for k in range(PER):
                at = (z * 2 + index) * PER + k
                codes = in_ref[0, z, index * ROWS : (index + 1) * ROWS, k * GROUP : (k + 1) * GROUP]
                served_ref[
                    index * ROWS : (index + 1) * ROWS, z * PART + k * GROUP : z * PART + (k + 1) * GROUP
                ] = (codes.astype(f32) * columns[:ROWS, at : at + 1]).astype(bf16)


def serve(half, place, strips, turned):
    return pl.pallas_call(
        serve_kernel,
        out_shape=(
            jax.ShapeDtypeStruct((N_Q * 2 * ROWS, Z_HALF * PART), bf16),
            jax.ShapeDtypeStruct((N_Z, N_Q, ROWS, PART), bf16),
            jax.ShapeDtypeStruct((N_Z, N_Q, STRIP - ROWS, PART), bf16),
        ),
        grid_spec=pltpu.PrefetchScalarGridSpec(
            num_scalar_prefetch=1,
            grid=(N_Q,),
            in_specs=[pl.BlockSpec((1, Z_HALF, STRIP, PART), lambda s, place: (s ^ place[1], 0, 0, 0))]
            + [pl.BlockSpec(memory_space=pl.ANY)] * len(turned),
            out_specs=(
                pl.BlockSpec((2 * ROWS, Z_HALF * PART), lambda s, place: (s, 0)),
                pl.BlockSpec((Z_HALF, 1, ROWS, PART), lambda s, place: (half, s ^ place[1], 0, 0)),
                pl.BlockSpec((Z_HALF, 1, STRIP - ROWS, PART), lambda s, place: (half, s ^ place[1], 0, 0)),
            ),
            scratch_shapes=[pltpu.VMEM((GROUP, GROUP), f32)],
        ),
        input_output_aliases={2 + n: 1 + n for n in range(len(turned))},
        compiler_params=params(),
        name="serve_gate_up",
    )(place, strips, *turned)


SPLIT = 4


def split_kernel(gate_in, up_in, gate_ref, gate_scales, up_ref, up_scales, gathered):
    columns = scale_columns(lambda n: up_in[n, ROWS:, :], SPLIT, gathered)
    for n in range(SPLIT):
        gate_ref[n * ROWS : (n + 1) * ROWS, :] = gate_in[n]
        up_ref[n * ROWS : (n + 1) * ROWS, :] = up_in[n, :ROWS]
        for index, scales in enumerate((gate_scales, up_scales)):
            at = (n * 2 + index) * PER
            scales[n * ROWS : (n + 1) * ROWS, :] = columns[:ROWS, at : at + PER]


def split(gate, up):
    codes = jax.ShapeDtypeStruct((FT, PART), bf16)
    scales = jax.ShapeDtypeStruct((FT, PER), f32)
    rows = SPLIT * ROWS
    return pl.pallas_call(
        split_kernel,
        out_shape=(codes, scales, codes, scales),
        grid=(N_TRAIN // SPLIT,),
        in_specs=[
            pl.BlockSpec((SPLIT, ROWS, PART), lambda s: (s, 0, 0)),
            pl.BlockSpec((SPLIT, STRIP - ROWS, PART), lambda s: (s, 0, 0)),
        ],
        out_specs=(
            pl.BlockSpec((rows, PART), lambda s: (s, 0)),
            pl.BlockSpec((rows, PER), lambda s: (s, 0)),
            pl.BlockSpec((rows, PART), lambda s: (s, 0)),
            pl.BlockSpec((rows, PER), lambda s: (s, 0)),
        ),
        scratch_shapes=[pltpu.VMEM((GROUP, GROUP), f32)],
        compiler_params=params(),
        name="split_gate_up",
    )(gate.reshape(N_TRAIN, ROWS, PART), up.reshape(N_TRAIN, STRIP - ROWS, PART))


def two_parts(row):
    high = row.astype(bf16).astype(f32)
    at = lax.broadcasted_iota(jnp.int32, (BLOCK, row.shape[1]), 0)
    return jnp.where(at == 0, high, jnp.where(at == 1, row - high, 0.0)).astype(bf16)


def message_of(state, gain):
    return (state * gain).astype(bf16), two_parts(jnp.sum(state * state, axis=0, keepdims=True))


SMEM_SPEC = pl.BlockSpec(memory_space=pltpu.SMEM)
VMEM_SPEC = pl.BlockSpec(memory_space=pltpu.VMEM)
ANY_SPEC = pl.BlockSpec(memory_space=pl.ANY)


def half_of(core):
    return pl.ds(pl.multiple_of(core * HALF, HALF), HALF)


def begin_kernel(place_ref, state_ref, gain_ref, heads_ref, state_out, out_ref):
    del heads_ref
    half = state_ref[half_of(place_ref[2]), :].astype(f32).T
    state_out[...] = half.astype(bf16)
    scaled, squares = message_of(half, gain_ref[...])
    for n in range(N_TRAIN):
        out_ref[n, :PART, :] = scaled
        out_ref[n, PART:, :] = squares


def begin(place, state, gain, heads):
    return pl.pallas_call(
        begin_kernel,
        out_shape=(
            jax.ShapeDtypeStruct((PART, HALF), bf16),
            jax.ShapeDtypeStruct((N_TRAIN, MSG, HALF), bf16),
        ),
        in_specs=[SMEM_SPEC, VMEM_SPEC, VMEM_SPEC, ANY_SPEC],
        compiler_params=params(),
        name="begin",
    )(place, state, gain, heads)


def release_kernel(*refs):
    del refs


def release(*arrays):
    return pl.pallas_call(
        release_kernel,
        out_shape=[jax.ShapeDtypeStruct(a.shape, a.dtype) for a in arrays],
        in_specs=[ANY_SPEC] * len(arrays),
        out_specs=[ANY_SPEC] * len(arrays),
        input_output_aliases={n: n for n in range(len(arrays))},
        compiler_params=params(),
        name="release",
    )(*arrays)


def activated(total, squares, width):
    inverse = lax.rsqrt(squares / width + EPSILON_NORM)
    gate = total[:ROWS] * inverse
    up = total[ROWS : 2 * ROWS] * inverse
    return (gate / (1.0 + jnp.exp(-gate)) * up).astype(bf16)


FIRST = 4


def first_kernel(width, place_ref, low_ref, high_ref, own_ref, other_ref, out_ref, total, squares):
    step = pl.program_id(0)
    in_low = step < N_TRAIN // FIRST // 2

    @pl.when(step == 0)
    def _():
        total[...] = jnp.zeros_like(total)
        squares[...] = jnp.zeros_like(squares)

    for side, x_ref in enumerate((own_ref, other_ref)):
        lanes = slice(side * HALF, (side + 1) * HALF)
        inputs = jnp.concatenate([x_ref[n, :PART, :] for n in range(FIRST)], axis=0)
        for near, weight_ref in ((in_low, low_ref), (~in_low, high_ref)):

            @pl.when(near)
            def _():
                total[:, lanes] += jnp.dot(weight_ref[...], inputs, preferred_element_type=f32)

        for n in range(FIRST):
            tail = x_ref[n, PART:, :].astype(f32)
            squares[0:1, lanes] += tail[0:1] + tail[1:2]

    @pl.when(step == N_TRAIN // FIRST - 1)
    def _():
        hidden = activated(total[...], squares[0:1, :], width)
        core = place_ref[2]
        for side in range(2):
            at = pl.multiple_of((core ^ side) * HALF, HALF)
            out_ref[:, pl.ds(at, HALF)] = hidden[:, side * HALF : (side + 1) * HALF]


def first_hidden(place, low, high, own, other, width):
    inputs = pl.BlockSpec((FIRST, MSG, HALF), lambda s, place: (s, 0, 0))
    steps = N_TRAIN // FIRST
    return pl.pallas_call(
        functools.partial(first_kernel, float(width)),
        out_shape=jax.ShapeDtypeStruct((ROWS, TOK), bf16),
        grid_spec=pltpu.PrefetchScalarGridSpec(
            num_scalar_prefetch=1,
            grid=(steps,),
            in_specs=[
                pl.BlockSpec((2 * ROWS, FIRST * PART), lambda s, place: (0, jnp.minimum(s, steps // 2 - 1))),
                pl.BlockSpec((2 * ROWS, FIRST * PART), lambda s, place: (0, jnp.maximum(s - steps // 2, 0))),
                inputs,
                inputs,
            ],
            out_specs=pl.BlockSpec((ROWS, TOK), lambda s, place: (0, 0)),
            scratch_shapes=[pltpu.VMEM((2 * ROWS, TOK), f32), pltpu.VMEM((8, TOK), f32)],
        ),
        compiler_params=params(),
        name="first_hidden",
    )(place, low, high, own, other)


def terms_kernel(place_ref, low_ref, high_ref, *refs):
    own, other, outs, inputs = refs[:N_Z], refs[N_Z : 2 * N_Z], refs[-N_Q - 2 : -2], refs[-1]
    core = place_ref[2]
    squares = []
    for side, messages in enumerate((own, other)):
        lanes = half_of(core ^ side)
        total = jnp.zeros((1, HALF), f32)
        for d, message in enumerate(messages):
            at = pl.multiple_of(lax.rem(place_ref[0] - d + N_Z, N_Z) * PART, PART)
            inputs[pl.ds(at, PART), lanes] = message[:PART, :]
            tail = message[PART:, :].astype(f32)
            total += tail[0:1] + tail[1:2]
        squares.append(total)
    middle = Z_HALF * PART
    for d, out in enumerate(outs):
        rows = slice(d * 2 * ROWS, (d + 1) * 2 * ROWS)
        total = jnp.dot(low_ref[rows, :], inputs[:middle, :], preferred_element_type=f32)
        total += jnp.dot(high_ref[rows, :], inputs[middle:, :], preferred_element_type=f32)
        out[: 2 * ROWS, :] = total.astype(bf16)
        for side in range(2):
            out[2 * ROWS :, half_of(core ^ side)] = two_parts(squares[side])


def gate_up_terms(place, low, high, own, other, held):
    return pl.pallas_call(
        terms_kernel,
        out_shape=[jax.ShapeDtypeStruct((STRIP, TOK), bf16)] * N_Q
        + [jax.ShapeDtypeStruct(held.shape, held.dtype)],
        in_specs=[SMEM_SPEC] + [VMEM_SPEC] * (2 + 2 * N_Z) + [ANY_SPEC],
        out_specs=[VMEM_SPEC] * N_Q + [ANY_SPEC],
        scratch_shapes=[pltpu.VMEM((N_Z * PART, TOK), bf16)],
        input_output_aliases={3 + 2 * N_Z: N_Q},
        compiler_params=params(),
        name="gate_up_terms",
    )(place, low, high, *own, *other, held)


def hidden_kernel(width, *refs):
    total = refs[0][...].astype(f32)
    for term in refs[1:-1]:
        total += term[...].astype(f32)
    squares = total[2 * ROWS : 2 * ROWS + 1] + total[2 * ROWS + 1 : 2 * ROWS + 2]
    refs[-1][...] = activated(total, squares, width)


def hidden_of(terms, width):
    return pl.pallas_call(
        functools.partial(hidden_kernel, float(width)),
        out_shape=jax.ShapeDtypeStruct((ROWS, TOK), bf16),
        compiler_params=params(),
        name="hidden",
    )(*terms)


def update_kernel(place_ref, *refs):
    hidden, weights = refs[:N_Q], refs[N_Q : N_Q + N_Z]
    keep_ref, send_ref, joined, result = refs[-4:]
    for d, block in enumerate(hidden):
        at = pl.multiple_of((place_ref[1] ^ d) * ROWS, BLOCK)
        joined[pl.ds(at, ROWS), :] = block[...]
    core = place_ref[2]
    for d, weight in enumerate(weights):
        result[d] = jnp.dot(weight[...], joined[...], preferred_element_type=f32).astype(bf16)
        keep_ref[d] = result[d, :, half_of(core)]
        send_ref[d] = result[d, :, half_of(core ^ 1)]


def update_terms(place, hidden, weights):
    return pl.pallas_call(
        update_kernel,
        out_shape=[jax.ShapeDtypeStruct((N_Z, PART, HALF), bf16)] * 2,
        in_specs=[SMEM_SPEC] + [VMEM_SPEC] * (N_Q + N_Z),
        scratch_shapes=[pltpu.VMEM((FT // N_Z, TOK), bf16), pltpu.VMEM((N_Z, PART, TOK), bf16)],
        compiler_params=params(),
        name="update_terms",
    )(place, *hidden, *weights)


def pair_kernel(own_ref, other_ref, *refs):
    for d, out in enumerate(refs[-N_Z:]):
        out[...] = (own_ref[d].astype(f32) + other_ref[d].astype(f32)).astype(bf16)


def pair_sums(own, other, after):
    return pl.pallas_call(
        pair_kernel,
        out_shape=[jax.ShapeDtypeStruct((PART, HALF), bf16)] * N_Z,
        in_specs=[VMEM_SPEC, VMEM_SPEC] + [ANY_SPEC] * len(after),
        compiler_params=params(),
        name="pair_sums",
    )(own, other, *after)


def sum_kernel(*refs):
    total = refs[0][...].astype(f32)
    for term in refs[1:-1]:
        total += term[...].astype(f32)
    refs[-1][...] = total.astype(bf16)


def sum_of(terms):
    return pl.pallas_call(
        sum_kernel,
        out_shape=jax.ShapeDtypeStruct((PART, HALF), bf16),
        compiler_params=params(),
        name="sum_over_z",
    )(*terms)


def advance_kernel(state_ref, own_ref, other_ref, gain_ref, next_ref, msg_ref):
    update = own_ref[...].astype(f32) + other_ref[...].astype(f32)
    state = (state_ref[...].astype(f32) + update).astype(bf16)
    next_ref[...] = state
    scaled, squares = message_of(state.astype(f32), gain_ref[...])
    msg_ref[:PART, :] = scaled
    msg_ref[PART:, :] = squares


def advance(state, own, other, gain):
    return pl.pallas_call(
        advance_kernel,
        out_shape=(jax.ShapeDtypeStruct((PART, HALF), bf16), jax.ShapeDtypeStruct((MSG, HALF), bf16)),
        compiler_params=params(),
        name="advance",
    )(state, own, other, gain)


def finish_kernel(place_ref, *refs):
    out_ref = refs[-1]
    for side in range(2):
        state, own, other = refs[3 * side : 3 * side + 3]
        update = own[...].astype(f32) + other[...].astype(f32)
        out_ref[half_of(place_ref[2] ^ side), :] = (state[...].astype(f32) + update).T.astype(bf16)


def finish(place, *sides):
    return pl.pallas_call(
        finish_kernel,
        out_shape=jax.ShapeDtypeStruct((TOK, PART), bf16),
        in_specs=[SMEM_SPEC] + [VMEM_SPEC] * 6,
        compiler_params=params(),
        name="finish",
    )(place, *sides)


def along_z(block, d):
    route = [(z * N_Q + q, (z + d) % N_Z * N_Q + q) for z in range(N_Z) for q in range(N_Q)]
    return lax.ppermute(block, "train", route)


def across_q(block, d):
    return lax.ppermute(block, "train", [(i, i ^ d) for i in range(N_TRAIN)])


def across_tp(block, d):
    return lax.ppermute(block, "tp", [(t, t ^ d) for t in range(4)])


def body(offsets, gate_flat, up_flat, down_flat, norm_gain, decode_state):
    width = norm_gain.shape[0]
    index = lax.axis_index("train")
    place = jnp.stack([index // N_Q, index % N_Q, lax.axis_index("tp") % 2]).astype(jnp.int32)
    q_groups = [[z * N_Q + q for q in range(N_Q)] for z in range(N_Z)]
    z_groups = [[z * N_Q + q for z in range(N_Z)] for q in range(N_Q)]

    heads = jnp.concatenate(
        [gate_flat[:, :GROUP], up_flat[:, :GROUP], down_flat[:, :GROUP], jnp.zeros((5, GROUP), f32)]
    )
    heads = lax.ppermute(heads, "train", [((i + 1) % N_TRAIN, i) for i in range(N_TRAIN)])
    gain = lax.dynamic_slice_in_dim(norm_gain, index * PART, PART, 0).reshape(PART, 1)
    state, first = begin(place, decode_state, gain, heads)
    first = lax.all_to_all(first, "train", 0, 0, tiled=True)

    gate, up, down = (flat.reshape(-1, GROUP) for flat in (gate_flat, up_flat, down_flat))
    low_strips, low_first = pack(0, offsets, gate, up, heads)
    high_strips, high_first = pack(Z_HALF, offsets, gate, up, heads)
    down_codes, down_scales, down_served = code_down(offsets, place, down, heads)
    first, low_strips, down_served = release(first, low_strips, down_served)
    low_strips = lax.all_to_all(low_strips, "train", 0, 0, axis_index_groups=q_groups, tiled=True)
    down_weights = [down_served[0]] + [along_z(down_served[d], d) for d in range(1, N_Z)]
    hidden = first_hidden(place, low_first, high_first, first, across_tp(first, 1), width)
    hidden, low_strips = release(hidden, low_strips)

    owned = []
    for step in range(STEPS):
        if step > 0:
            own = [message] + [along_z(message, d) for d in range(1, N_Z)]
            other = [across_tp(m, 1) for m in own]
            *terms, held = gate_up_terms(place, low_served, high_served, own, other, turned[step - 1])
            owned.append(lax.all_to_all(held, "train", 0, 0, axis_index_groups=z_groups, tiled=True))
            hidden = hidden_of([terms[0]] + [across_q(terms[d], d) for d in range(1, N_Q)], width)
        blocks = [hidden] + [across_q(hidden, d) for d in range(1, N_Q)]
        keep, send = update_terms(place, blocks, down_weights)
        if step == 0:
            keep, high_strips = release(keep, high_strips)
            high_strips = lax.all_to_all(high_strips, "train", 0, 0, axis_index_groups=q_groups, tiled=True)
            low_served, *turned = serve(0, place, low_strips, ())
            high_served, *turned = serve(1, place, high_strips, turned)
        sums = pair_sums(keep, across_tp(send, 1), owned[-1:])
        own = sum_of([sums[0]] + [along_z(sums[d], -d) for d in range(1, N_Z)])
        if step < STEPS - 1:
            state, message = advance(state, own, across_tp(own, 2), gain)
        else:
            decoded = finish(
                place, state, own, across_tp(own, 2), across_tp(state, 1), across_tp(own, 1), across_tp(own, 3)
            )
    gate_codes, gate_scales, up_codes, up_scales = split(*owned)
    return (gate_codes, gate_scales, up_codes, up_scales, down_codes, down_scales, decoded)


def solution(mesh):
    in_specs = (P(), P("tp", "train"), P("tp", "train"), P("tp", "train"), P(), P(None, "train"))
    out_specs = (
        P("tp", "train"),
        P("tp", "train"),
        P("tp", "train"),
        P("tp", "train"),
        P("train", "tp"),
        P("train", "tp"),
        P(None, "train"),
    )
    return jax.shard_map(body, mesh=mesh, in_specs=in_specs, out_specs=out_specs, check_vma=False)
```

time: 1440 us -> 393 us (0.27)
  waiting for transfers between devices: 939 us -> 87.3 us
  blocking collectives: 210 us -> 0 us
  starting transfers between devices: 28.4 us -> 142 us
  other arithmetic: 86.8 us -> 0.15 us
  Pallas kernels: 0 us -> 85.4 us
  local copies, waits for them, and re-layouts: 129 us -> 68.9 us
  matrix products: 18.9 us -> 0 us
  between operations: 20.5 us -> 1.61 us
    all_gather x3 -> x0, waiting for transfers between devices: 415 us -> none  [body(): lax.all_gather(hidden, 'train', axis=0, tiled=True)]
    unnamed x12 -> x0, waiting for transfers between devices: 250 us -> none
    psum x3 -> x0, blocking collectives: 210 us -> none  [body(): squares = lax.psum(jnp.sum(wide_state * wide_state, axis=1), 'train')]
    psum x3 -> x0, waiting for transfers between devices: 187 us -> none  [body(): update = lax.psum(partial_update, 'tp')]
    ppermute x3 -> x72, starting transfers between devices: 9.56 us -> 116 us  [the longest x35 52.4 us: across_q(): return lax.ppermute(block, 'train', [(i, i ^ d) for i in range(N_TRAIN)])]
    pallas_call x0 -> x27, Pallas kernels: none -> 85.4 us  [the longest x2 22.8 us: pack(): pl.pallas_call(functools.partial(pack_kernel, z_first), out_shape=(jax.Sh...]
    all_to_all x2 -> x5, waiting for transfers between devices: 87.9 us -> 10 us  [the longest x1 6.45 us: body(): first = lax.all_to_all(first, 'train', 0, 0, tiled=True)]
    ppermute x3 -> x72, waiting for transfers between devices: 0.01 us -> 77.3 us  [the longest x18 27.9 us: across_tp(): return lax.ppermute(block, 'tp', [(t, t ^ d) for t in range(4)])]
  transfers between devices with their start and end apart: 14 -> 77, of which waited for: 11 -> 34; matrix products, arithmetic and copies ran while one was open for 8% -> 3% of each run, Pallas kernels for 0% -> 19%
where the time goes in v1:
time: 393 us; the launch traced here: 386 us
  starting transfers between devices  142 us (36%)
  waiting for transfers between devices  87.3 us (22%)
  Pallas kernels  85.4 us (22%)
  local copies, waits for them, and re-layouts  68.9 us (18%)
    unnamed x125, local copies, waits for them, and re-layouts  62.6 us
    ppermute x35, starting transfers between devices, across_q(): return lax.ppermute(block, 'train', [(i, i ^ d) for i in range(N_TRAIN)])  52.4 us
    ppermute x18, starting transfers between devices, across_tp(): return lax.ppermute(block, 'tp', [(t, t ^ d) for t in range(4)])  35.8 us
    ppermute x18, waiting for transfers between devices, across_tp(): return lax.ppermute(block, 'tp', [(t, t ^ d) for t in range(4)])  27.9 us
    ppermute x35, waiting for transfers between devices, across_q(): return lax.ppermute(block, 'train', [(i, i ^ d) for i in range(N_TRAIN)])  27.8 us
    pallas_call x2, Pallas kernels, pack(): pl.pallas_call(functools.partial(pack_kernel, z_first), out_shape=(jax.Sh...  22.8 us
    ppermute x18, waiting for transfers between devices, along_z(): return lax.ppermute(block, 'train', route)  21.5 us
    ppermute x18, starting transfers between devices, along_z(): return lax.ppermute(block, 'train', route)  19.5 us
  transfers between devices with their start and end apart: 77, of which 34 were waited for; matrix products, arithmetic and copies ran while one was open for 3% of the time, Pallas kernels for 19%

profile of v1, /device:TPU:1, one launch (start us, length us, event | category | flops | bytes accessed | tf_op | source)
XLA Modules:
  0.0 385.7 jit_solution(17387713773504194195)
XLA Ops:
  2.8 7.8 %collective-permute-start = (f32[8,128]{1,0:T(8,128)S(1)}, f32[8,128]{1,0:T(8,128)S(1)}, u32[]{:S(2)}, u32[]{:S(2)}) collective-permute-start(f32[8,128]{1,0:T(8,128)S(1)} %maximum_maximum_fusion), channel_id=1, source_target_pairs={{4,0},{8,4},{12,8},{16,12},{20,16},{24,20},{28,24},{32,28},{36,32}... | collective-permute-start | bytes 12296 | tf_op jit(solution)/shard_map/ppermute | solution.py:579
  15.7 7.5 %all-to-all-start = ((bf16[32,400,128]{2,1,0:T(8,128)(2,1)}), bf16[32,400,128]{2,1,0:T(8,128)(2,1)S(1)}, u32[]{:S(2)}, u32[]{:S(2)}) async-start(bf16[32,400,128]{2,1,0:T(8,128)(2,1)} %copy-done.24), calls=%async_computation | async-start | bytes 6553600 | tf_op jit(solution)/shard_map/all_to_all | solution.py:582
  26.0 15.3 %code_down.1 = (bf16[384,3584]{1,0:T(8,128)(2,1)}, f32[384,28]{1,0:T(8,128)S(1)}, bf16[4,384,896]{2,1,0:T(8,128)(2,1)S(1)}) custom-call(s32[3]{0:T(128)S(1)} %copy-done.46, s32[3]{0:T(128)S(1)} %pad_add_fusion.place_ref, f32[10752,128]{1,0:T(8,128)S(1)} %bitcast.27, f32[10752,128]{1,0:T(8,128)S(1)} %bitcast.28, f32[8,128]{1,0:T(8,128)S(1)} %collective-permute-done.heads_ref), custom_call_target="tpu_custom_call" | custom-call | tf_op jit(solution)/shard_map/code_down/pallas_call | solution.py:172
  43.4 11.0 %pack_gate_up.2 = (bf16[8,2,240,384]{3,2,1,0:T(8,128)(2,1)S(1)}, bf16[224,6144]{1,0:T(8,128)(2,1)S(1)}) custom-call(s32[3]{0:T(128)S(1)} %copy-done.46, f32[112,96,128]{2,1,0:T(8,128)S(1)} %bitcast.18, f32[112,96,128]{2,1,0:T(8,128)S(1)} %bitcast.19, f32[112,96,128]{2,1,0:T(8,128)S(1)} %bitcast.22, f32[112,96,128]{2,1,0:T(8,128)S(1)} %bitcast.23, ...), custom_call_target="tpu_custom_call" | custom-call | tf_op jit(solution)/shard_map/pack_gate_up/pallas_call | solution.py:127
  57.7 6.4 %all-to-all-done.refs_0_ = bf16[32,400,128]{2,1,0:T(8,128)(2,1)S(1)} async-done(((bf16[32,400,128]{2,1,0:T(8,128)(2,1)}), bf16[32,400,128]{2,1,0:T(8,128)(2,1)S(1)}, u32[]{:S(2)}, u32[]{:S(2)}) %all-to-all-start) | async-done | bytes 3276832 | tf_op jit(solution)/shard_map/all_to_all | solution.py:582
  72.0 6.4 %all-to-all-start.1 = ((bf16[8,2,240,384]{3,2,1,0:T(8,128)(2,1)}), bf16[8,2,240,384]{3,2,1,0:T(8,128)(2,1)}, u32[]{:S(2)}, u32[]{:S(2)}) async-start(bf16[8,2,240,384]{3,2,1,0:T(8,128)(2,1)} %copy-done.12), calls=%async_computation.1 | async-start | bytes 5898240 | tf_op jit(solution)/shard_map/all_to_all | solution.py:589
  90.6 11.8 %pack_gate_up.3 = (bf16[8,2,240,384]{3,2,1,0:T(8,128)(2,1)}, bf16[224,6144]{1,0:T(8,128)(2,1)S(1)}) custom-call(s32[3]{0:T(128)S(1)} %copy-done.46, f32[112,96,128]{2,1,0:T(8,128)S(1)} %bitcast.20, f32[112,96,128]{2,1,0:T(8,128)S(1)} %bitcast.21, f32[112,96,128]{2,1,0:T(8,128)S(1)} %bitcast.24, f32[112,96,128]{2,1,0:T(8,128)S(1)} %bitcast.25, ...), custom_call_target="tpu_custom_call" | custom-call | tf_op jit(solution)/shard_map/pack_gate_up/pallas_call | solution.py:127
  102.4 8.7 %first_hidden.1.refs_0_ = bf16[112,256]{1,0:T(8,128)(2,1)S(1)} custom-call(s32[3]{0:T(128)S(1)} %pad_add_fusion.place_ref, bf16[224,6144]{1,0:T(8,128)(2,1)S(1)} %copy-done.26, bf16[224,6144]{1,0:T(8,128)(2,1)S(1)} %get-tuple-element.74.high_ref, bf16[32,400,128]{2,1,0:T(8,128)(2,1)S(1)} %get-tuple-element.78.own_ref, ...), custom_call_target="tpu_custom_call" | custom-call | tf_op jit(solution)/shard_map/first_hidden/pallas_call | solution.py:391
  111.1 3.6 all-to-all-done.1.refs_1_
  114.7 4.3 %collective-permute-start.3 = (bf16[112,256]{1,0:T(8,128)(2,1)S(1)}, bf16[112,256]{1,0:T(8,128)(2,1)S(1)}, u32[]{:S(2)}, u32[]{:S(2)}) collective-permute-start(bf16[112,256]{1,0:T(8,128)(2,1)S(1)} %get-tuple-element.82.refs_0_), channel_id=1, source_target_pairs={{0,8},{4,12},{8,0},{12,4},{16,24},{20,28},{24,16},{28,20},{32,40},... | collective-permute-start | bytes 172040 | tf_op jit(solution)/shard_map/ppermute | solution.py:562
  118.9 4.1 %collective-permute-start.5 = (bf16[112,256]{1,0:T(8,128)(2,1)S(1)}, bf16[112,256]{1,0:T(8,128)(2,1)S(1)}, u32[]{:S(2)}, u32[]{:S(2)}) collective-permute-start(bf16[112,256]{1,0:T(8,128)(2,1)S(1)} %get-tuple-element.82.refs_0_), channel_id=1, source_target_pairs={{0,16},{4,20},{8,24},{12,28},{16,0},{20,4},{24,8},{28,12},{32,48},... | collective-permute-start | bytes 172040 | tf_op jit(solution)/shard_map/ppermute | solution.py:562
  123.0 4.7 %collective-permute-start.7 = (bf16[112,256]{1,0:T(8,128)(2,1)S(1)}, bf16[112,256]{1,0:T(8,128)(2,1)S(1)}, u32[]{:S(2)}, u32[]{:S(2)}) collective-permute-start(bf16[112,256]{1,0:T(8,128)(2,1)S(1)} %get-tuple-element.82.refs_0_), channel_id=1, source_target_pairs={{0,24},{4,28},{8,16},{12,20},{16,8},{20,12},{24,0},{28,4},{32,56},... | collective-permute-start | bytes 172040 | tf_op jit(solution)/shard_map/ppermute | solution.py:562
  135.6 4.6 %all-to-all-start.2 = ((bf16[8,2,240,384]{3,2,1,0:T(8,128)(2,1)}), bf16[8,2,240,384]{3,2,1,0:T(8,128)(2,1)}, u32[]{:S(2)}, u32[]{:S(2)}) async-start(bf16[8,2,240,384]{3,2,1,0:T(8,128)(2,1)} %get-tuple-element.86), calls=%async_computation.2 | async-start | bytes 5898240 | tf_op jit(solution)/shard_map/all_to_all | solution.py:606
  140.2 5.8 %collective-permute-start.12 = (bf16[4,384,128]{2,1,0:T(8,128)(2,1)S(1)}, bf16[4,384,128]{2,1,0:T(8,128)(2,1)S(1)}, u32[]{:S(2)}, u32[]{:S(2)}) collective-permute-start(bf16[4,384,128]{2,1,0:T(8,128)(2,1)S(1)} %get-tuple-element.92), channel_id=1, source_target_pairs={{0,1},{1,0},{2,3},{3,2},{4,5},{5,4},{6,7},{7,6},{8,9},{9,8},{10,11... | collective-permute-start | bytes 1179656 | tf_op jit(solution)/shard_map/ppermute | solution.py:566
  159.6 18.9 %collective-permute-done.16.other_ref = bf16[384,128]{1,0:T(8,128)(2,1)S(1)} collective-permute-done((bf16[384,128]{1,0:T(8,128)(2,1)S(1)}, bf16[384,128]{1,0:T(8,128)(2,1)S(1)}, u32[]{:S(2)}, u32[]{:S(2)}) %collective-permute-start.16) | collective-permute-done | bytes 98336 | tf_op jit(solution)/shard_map/ppermute | solution.py:566
  188.8 6.9 %serve_gate_up.2 = (bf16[1792,768]{1,0:T(8,128)(2,1)S(1)}, bf16[4,8,112,384]{3,2,1,0:T(8,128)(2,1)S(1)}, bf16[4,8,128,384]{3,2,1,0:T(8,128)(2,1)S(1)}) custom-call(s32[3]{0:T(128)S(1)} %pad_add_fusion.place_ref, bf16[8,2,240,384]{3,2,1,0:T(8,128)(2,1)} %get-tuple-element.80.in_ref), custom_call_target="tpu_custom_call" | custom-call | tf_op jit(solution)/shard_map/serve_gate_up/pallas_call | solution.py:227
  200.6 7.2 %serve_gate_up.3 = (bf16[1792,768]{1,0:T(8,128)(2,1)S(1)}, bf16[4,8,112,384]{3,2,1,0:T(8,128)(2,1)S(1)}, bf16[4,8,128,384]{3,2,1,0:T(8,128)(2,1)S(1)}) custom-call(s32[3]{0:T(128)S(1)} %pad_add_fusion.place_ref, bf16[8,2,240,384]{3,2,1,0:T(8,128)(2,1)} %all-to-all-done.2.in_ref, ...), custom_call_target="tpu_custom_call", output_to_operand_aliasing={{1}: (2, {}), {2}: (3, {})} | custom-call | tf_op jit(solution)/shard_map/serve_gate_up/pallas_call | solution.py:227
  222.0 4.6 %all-to-all-start.3 = ((bf16[4,8,112,384]{3,2,1,0:T(8,128)(2,1)}), bf16[4,8,112,384]{3,2,1,0:T(8,128)(2,1)}, u32[]{:S(2)}, u32[]{:S(2)}) async-start(bf16[4,8,112,384]{3,2,1,0:T(8,128)(2,1)} %copy-done.8), calls=%async_computation.3 | async-start | bytes 5505024 | tf_op jit(solution)/shard_map/all_to_all | solution.py:600
  239.4 3.8 collective-permute-done.30.refs_7_
  249.1 4.2 %collective-permute-start.36 = (bf16[112,256]{1,0:T(8,128)(2,1)S(1)}, bf16[112,256]{1,0:T(8,128)(2,1)S(1)}, u32[]{:S(2)}, u32[]{:S(2)}) collective-permute-start(bf16[112,256]{1,0:T(8,128)(2,1)S(1)} %hidden.2.refs_0_), channel_id=1, source_target_pairs={{0,24},{4,28},{8,16},{12,20},{16,8},{20,12},{24,0},{28,4},{32,56},... | collective-permute-start | bytes 172040 | tf_op jit(solution)/shard_map/ppermute | solution.py:562
  282.4 4.0 %collective-permute-done.42.other_ref = bf16[384,128]{1,0:T(8,128)(2,1)S(1)} collective-permute-done((bf16[384,128]{1,0:T(8,128)(2,1)S(1)}, bf16[384,128]{1,0:T(8,128)(2,1)S(1)}, u32[]{:S(2)}, u32[]{:S(2)}) %collective-permute-start.42) | collective-permute-done | bytes 98336 | tf_op jit(solution)/shard_map/ppermute | solution.py:566
  307.9 3.7 all-to-all-start.4
  339.1 3.8 collective-permute-done.63.refs_7_
  369.9 7.1 %split_gate_up.1 = (bf16[3584,384]{1,0:T(8,128)(2,1)}, f32[3584,3]{1,0:T(8,128)S(1)}, bf16[3584,384]{1,0:T(8,128)(2,1)}, f32[3584,3]{1,0:T(8,128)S(1)}) custom-call(bf16[32,112,384]{2,1,0:T(8,128)(2,1)} %bitcast.10.gate_in, bf16[32,128,384]{2,1,0:T(8,128)(2,1)S(1)} %bitcast.26), custom_call_target="tpu_custom_call" | custom-call | tf_op jit(solution)/shard_map/split_gate_up/pallas_call | solution.py:269
  (293 shorter events, 218.1 us)
Async XLA Ops:
  15.7 48.4 %all-to-all-start = ((bf16[32,400,128]{2,1,0:T(8,128)(2,1)}), bf16[32,400,128]{2,1,0:T(8,128)(2,1)S(1)}, u32[]{:S(2)}, u32[]{:S(2)}) async-start(bf16[32,400,128]{2,1,0:T(8,128)(2,1)} %copy-done.24), calls=%async_computation | async-start | bytes 6553600 | tf_op jit(solution)/shard_map/all_to_all | solution.py:582
  69.3 33.1 %collective-permute-start.1 = (bf16[32,400,128]{2,1,0:T(8,128)(2,1)S(1)}, bf16[32,400,128]{2,1,0:T(8,128)(2,1)}, u32[]{:S(2)}, u32[]{:S(2)}) collective-permute-start(bf16[32,400,128]{2,1,0:T(8,128)(2,1)S(1)} %get-tuple-element.78.own_ref), channel_id=1, source_target_pairs={{0,1},{1,0},{2,3},{3,2},{4,5},{5,4},{6,7},{7,6},{8,9},{9,8},{10,11... | collective-permute-start | bytes 9830408 | tf_op jit(solution)/shard_map/ppermute | solution.py:566
  72.0 42.7 %all-to-all-start.1 = ((bf16[8,2,240,384]{3,2,1,0:T(8,128)(2,1)}), bf16[8,2,240,384]{3,2,1,0:T(8,128)(2,1)}, u32[]{:S(2)}, u32[]{:S(2)}) async-start(bf16[8,2,240,384]{3,2,1,0:T(8,128)(2,1)} %copy-done.12), calls=%async_computation.1 | async-start | bytes 5898240 | tf_op jit(solution)/shard_map/all_to_all | solution.py:589
  81.7 37.2 %collective-permute-start.10 = (bf16[384,896]{1,0:T(8,128)(2,1)}, bf16[384,896]{1,0:T(8,128)(2,1)}, u32[]{:S(2)}, u32[]{:S(2)}) collective-permute-start(bf16[384,896]{1,0:T(8,128)(2,1)} %get-tuple-element.154), channel_id=1, source_target_pairs={{0,64},{4,68},{8,72},{12,76},{16,80},{20,84},{24,88},{28,92},{32,9... | collective-permute-start | bytes 2064392 | tf_op jit(solution)/shard_map/ppermute | solution.py:558
  82.8 36.1 %collective-permute-start.11 = (bf16[384,896]{1,0:T(8,128)(2,1)}, bf16[384,896]{1,0:T(8,128)(2,1)}, u32[]{:S(2)}, u32[]{:S(2)}) collective-permute-start(bf16[384,896]{1,0:T(8,128)(2,1)} %get-tuple-element.153), channel_id=1, source_target_pairs={{0,96},{4,100},{8,104},{12,108},{16,112},{20,116},{24,120},{28,124... | collective-permute-start | bytes 2064392 | tf_op jit(solution)/shard_map/ppermute | solution.py:558
  85.3 37.7 %collective-permute-start.9 = (bf16[384,896]{1,0:T(8,128)(2,1)}, bf16[384,896]{1,0:T(8,128)(2,1)}, u32[]{:S(2)}, u32[]{:S(2)}) collective-permute-start(bf16[384,896]{1,0:T(8,128)(2,1)} %get-tuple-element.155), channel_id=1, source_target_pairs={{0,32},{4,36},{8,40},{12,44},{16,48},{20,52},{24,56},{28,60},{32,6... | collective-permute-start | bytes 2064392 | tf_op jit(solution)/shard_map/ppermute | solution.py:558
  114.7 13.0 %collective-permute-start.3 = (bf16[112,256]{1,0:T(8,128)(2,1)S(1)}, bf16[112,256]{1,0:T(8,128)(2,1)S(1)}, u32[]{:S(2)}, u32[]{:S(2)}) collective-permute-start(bf16[112,256]{1,0:T(8,128)(2,1)S(1)} %get-tuple-element.82.refs_0_), channel_id=1, source_target_pairs={{0,8},{4,12},{8,0},{12,4},{16,24},{20,28},{24,16},{28,20},{32,40},... | collective-permute-start | bytes 172040 | tf_op jit(solution)/shard_map/ppermute | solution.py:562
  118.9 8.8 %collective-permute-start.4 = (bf16[112,256]{1,0:T(8,128)(2,1)S(1)}, bf16[112,256]{1,0:T(8,128)(2,1)S(1)}, u32[]{:S(2)}, u32[]{:S(2)}) collective-permute-start(bf16[112,256]{1,0:T(8,128)(2,1)S(1)} %get-tuple-element.82.refs_0_), channel_id=1, source_target_pairs={{0,12},{4,8},{8,4},{12,0},{16,28},{20,24},{24,20},{28,16},{32,44},... | collective-permute-start | bytes 172040 | tf_op jit(solution)/shard_map/ppermute | solution.py:562
  135.6 63.2 %all-to-all-start.2 = ((bf16[8,2,240,384]{3,2,1,0:T(8,128)(2,1)}), bf16[8,2,240,384]{3,2,1,0:T(8,128)(2,1)}, u32[]{:S(2)}, u32[]{:S(2)}) async-start(bf16[8,2,240,384]{3,2,1,0:T(8,128)(2,1)} %get-tuple-element.86), calls=%async_computation.2 | async-start | bytes 5898240 | tf_op jit(solution)/shard_map/all_to_all | solution.py:606
  156.9 21.6 %collective-permute-start.16 = (bf16[384,128]{1,0:T(8,128)(2,1)S(1)}, bf16[384,128]{1,0:T(8,128)(2,1)S(1)}, u32[]{:S(2)}, u32[]{:S(2)}) collective-permute-start(bf16[384,128]{1,0:T(8,128)(2,1)S(1)} %sum_over_z.3.own_ref), channel_id=1, source_target_pairs={{0,2},{1,3},{2,0},{3,1},{4,6},{5,7},{6,4},{7,5},{8,10},{9,11},{10,... | collective-permute-start | bytes 294920 | tf_op jit(solution)/shard_map/ppermute | solution.py:566
  179.3 8.8 %collective-permute-start.18 = (bf16[400,128]{1,0:T(8,128)(2,1)S(1)}, bf16[400,128]{1,0:T(8,128)(2,1)}, u32[]{:S(2)}, u32[]{:S(2)}) collective-permute-start(bf16[400,128]{1,0:T(8,128)(2,1)S(1)} %get-tuple-element.97.refs_0_), channel_id=1, source_target_pairs={{0,64},{4,68},{8,72},{12,76},{16,80},{20,84},{24,88},{28,92},{32,9... | collective-permute-start | bytes 307208 | tf_op jit(solution)/shard_map/ppermute | solution.py:558
  182.0 27.3 %collective-permute-start.20 = (bf16[400,128]{1,0:T(8,128)(2,1)S(1)}, bf16[400,128]{1,0:T(8,128)(2,1)}, u32[]{:S(2)}, u32[]{:S(2)}) collective-permute-start(bf16[400,128]{1,0:T(8,128)(2,1)S(1)} %get-tuple-element.97.refs_0_), channel_id=1, source_target_pairs={{0,1},{1,0},{2,3},{3,2},{4,5},{5,4},{6,7},{7,6},{8,9},{9,8},{10,11... | collective-permute-start | bytes 307208 | tf_op jit(solution)/shard_map/ppermute | solution.py:566
  186.2 23.1 %collective-permute-start.21 = (bf16[400,128]{1,0:T(8,128)(2,1)}, bf16[400,128]{1,0:T(8,128)(2,1)}, u32[]{:S(2)}, u32[]{:S(2)}) collective-permute-start(bf16[400,128]{1,0:T(8,128)(2,1)} %collective-permute-done.17.refs_1_), channel_id=1, source_target_pairs={{0,1},{1,0},{2,3},{3,2},{4,5},{5,4},{6,7},{7,6},{8,9},{9,8},{10,11... | collective-permute-start | bytes 307208 | tf_op jit(solution)/shard_map/ppermute | solution.py:566
  188.1 21.2 %collective-permute-start.22 = (bf16[400,128]{1,0:T(8,128)(2,1)}, bf16[400,128]{1,0:T(8,128)(2,1)}, u32[]{:S(2)}, u32[]{:S(2)}) collective-permute-start(bf16[400,128]{1,0:T(8,128)(2,1)} %collective-permute-done.18.refs_2_), channel_id=1, source_target_pairs={{0,1},{1,0},{2,3},{3,2},{4,5},{5,4},{6,7},{7,6},{8,9},{9,8},{10,11... | collective-permute-start | bytes 307208 | tf_op jit(solution)/shard_map/ppermute | solution.py:566
  188.3 21.0 %collective-permute-start.23 = (bf16[400,128]{1,0:T(8,128)(2,1)}, bf16[400,128]{1,0:T(8,128)(2,1)}, u32[]{:S(2)}, u32[]{:S(2)}) collective-permute-start(bf16[400,128]{1,0:T(8,128)(2,1)} %collective-permute-done.19.refs_3_), channel_id=1, source_target_pairs={{0,1},{1,0},{2,3},{3,2},{4,5},{5,4},{6,7},{7,6},{8,9},{9,8},{10,11... | collective-permute-start | bytes 307208 | tf_op jit(solution)/shard_map/ppermute | solution.py:566
  222.0 46.6 %all-to-all-start.3 = ((bf16[4,8,112,384]{3,2,1,0:T(8,128)(2,1)}), bf16[4,8,112,384]{3,2,1,0:T(8,128)(2,1)}, u32[]{:S(2)}, u32[]{:S(2)}) async-start(bf16[4,8,112,384]{3,2,1,0:T(8,128)(2,1)} %copy-done.8), calls=%async_computation.3 | async-start | bytes 5505024 | tf_op jit(solution)/shard_map/all_to_all | solution.py:600
  228.6 9.8 %collective-permute-start.26 = (bf16[240,256]{1,0:T(8,128)(2,1)}, bf16[240,256]{1,0:T(8,128)(2,1)S(1)}, u32[]{:S(2)}, u32[]{:S(2)}) collective-permute-start(bf16[240,256]{1,0:T(8,128)(2,1)} %copy-done.54), channel_id=1, source_target_pairs={{0,12},{4,8},{8,4},{12,0},{16,28},{20,24},{24,20},{28,16},{32,44},... | collective-permute-start | bytes 368648 | tf_op jit(solution)/shard_map/ppermute | solution.py:562
  288.0 8.9 %collective-permute-start.44 = (bf16[400,128]{1,0:T(8,128)(2,1)S(1)}, bf16[400,128]{1,0:T(8,128)(2,1)S(1)}, u32[]{:S(2)}, u32[]{:S(2)}) collective-permute-start(bf16[400,128]{1,0:T(8,128)(2,1)S(1)} %get-tuple-element.115.refs_0_), channel_id=1, source_target_pairs={{0,64},{4,68},{8,72},{12,76},{16,80},{20,84},{24,88},{28,92},{32,9... | collective-permute-start | bytes 307208 | tf_op jit(solution)/shard_map/ppermute | solution.py:558
  307.9 44.3 %all-to-all-start.4 = ((bf16[4,8,128,384]{3,2,1,0:T(8,128)(2,1)}), bf16[4,8,128,384]{3,2,1,0:T(8,128)(2,1)S(1)}, u32[]{:S(2)}, u32[]{:S(2)}) async-start(bf16[4,8,128,384]{3,2,1,0:T(8,128)(2,1)} %copy-done.3), calls=%async_computation.4 | async-start | bytes 6291456 | tf_op jit(solution)/shard_map/all_to_all | solution.py:600
  314.5 9.1 %collective-permute-start.52 = (bf16[240,256]{1,0:T(8,128)(2,1)}, bf16[240,256]{1,0:T(8,128)(2,1)S(1)}, u32[]{:S(2)}, u32[]{:S(2)}) collective-permute-start(bf16[240,256]{1,0:T(8,128)(2,1)} %copy-done.53), channel_id=1, source_target_pairs={{0,12},{4,8},{8,4},{12,0},{16,28},{20,24},{24,20},{28,16},{32,44},... | collective-permute-start | bytes 368648 | tf_op jit(solution)/shard_map/ppermute | solution.py:562
  357.3 26.1 %collective-permute-start.69 = (bf16[384,128]{1,0:T(8,128)(2,1)}, bf16[384,128]{1,0:T(8,128)(2,1)S(1)}, u32[]{:S(2)}, u32[]{:S(2)}) collective-permute-start(bf16[384,128]{1,0:T(8,128)(2,1)} %get-tuple-element.124.refs_0_), channel_id=1, source_target_pairs={{0,1},{1,0},{2,3},{3,2},{4,5},{5,4},{6,7},{7,6},{8,9},{9,8},{10,11... | collective-permute-start | bytes 294920 | tf_op jit(solution)/shard_map/ppermute | solution.py:566
  364.3 19.2 %collective-permute-start.68 = (bf16[384,128]{1,0:T(8,128)(2,1)S(1)}, bf16[384,128]{1,0:T(8,128)(2,1)S(1)}, u32[]{:S(2)}, u32[]{:S(2)}) collective-permute-start(bf16[384,128]{1,0:T(8,128)(2,1)S(1)} %sum_over_z.5.refs_1_), channel_id=1, source_target_pairs={{0,2},{1,3},{2,0},{3,1},{4,6},{5,7},{6,4},{7,5},{8,10},{9,11},{10,... | collective-permute-start | bytes 294920 | tf_op jit(solution)/shard_map/ppermute | solution.py:566
  365.6 17.9 %collective-permute-start.70 = (bf16[384,128]{1,0:T(8,128)(2,1)S(1)}, bf16[384,128]{1,0:T(8,128)(2,1)S(1)}, u32[]{:S(2)}, u32[]{:S(2)}) collective-permute-start(bf16[384,128]{1,0:T(8,128)(2,1)S(1)} %sum_over_z.5.refs_1_), channel_id=1, source_target_pairs={{0,1},{1,0},{2,3},{3,2},{4,5},{5,4},{6,7},{7,6},{8,9},{9,8},{10,11... | collective-permute-start | bytes 294920 | tf_op jit(solution)/shard_map/ppermute | solution.py:566
  366.6 16.9 %collective-permute-start.71 = (bf16[384,128]{1,0:T(8,128)(2,1)S(1)}, bf16[384,128]{1,0:T(8,128)(2,1)}, u32[]{:S(2)}, u32[]{:S(2)}) collective-permute-start(bf16[384,128]{1,0:T(8,128)(2,1)S(1)} %sum_over_z.5.refs_1_), channel_id=1, source_target_pairs={{0,3},{1,2},{2,1},{3,0},{4,7},{5,6},{6,5},{7,4},{8,11},{9,10},{10,... | collective-permute-start | bytes 294920 | tf_op jit(solution)/shard_map/ppermute | solution.py:566
  (114 other events, 630.6 us)
